TPU v7x, 32 devices: a whole 2x2x4 slice. The times are simulated.
32 devices in a mesh: grp: 4 (over y, x), slab: 8 (over z, core).
Axes of the slice: x: 2, y: 2, z: 4, core: 2. Of those that a mesh axis runs over, the one named last changes fastest.
Arguments:
- source: float32 [128, 32, 1024], P('grp', None, 'slab'), may hold values from -6 to 6
- occupancy: int32 [16, 4, 128], P('grp', None, 'slab'), may hold values 0 or 1
- classes: int32 [16, 4, 128], P('grp', None, 'slab'), may hold values from 0 to 15
- screen_table: float32 [16], replicated, may hold values from 0.5 to 8
- parents: int32 [8, 2, 64], P('grp', None, 'slab'), may hold values from 0 to 31, as said below
- coarse: float32 [4, 32, 512], P('grp', 'slab'), may hold values from -6 to 6
Outputs:
- middle_field: float32 [64, 16, 512], P('grp', None, 'slab')
- finest_field: float32 [128, 32, 1024], P('grp', None, 'slab')
Inputs may be any that keep to these rules, and one draw needn't show every extreme that they name: parents[I, J, K] is the position, in the list of the group that holds the brick, of the depth-12 brick containing depth-13 brick (I, J, K); each group's list holds each depth-12 brick of the group's region once, so each position is the parent of eight depth-13 bricks. The parent of a brick on slab index s lies in list positions [(s - 1) * 4, (s + 2) * 4).
All inputs are finite; a program needn't handle non-finite values. No bound on the sum of `occupancy` on one device may be relied on, other than what follows from the above.
Results may differ from a plain program's by a relative error of at most 0.00002.
Values sent between devices are 32-bit elements; how exact they have to be, the bound alone decides.
A program may use at most 128 MiB of HBM per device.

v0:
```python
import jax
import jax.numpy as jnp
from jax import lax
from jax.sharding import PartitionSpec as P

BRICK = 8
SWEEPS = 3


screen_strength = 4.0
relaxation = 2.0 / 3.0
stiff_diagonal = 8.0 / 3.0
mass_diagonal = 8.0 / 27.0


def extended(block, sides, width):
    for axis, dim in sides:
        count = lax.axis_size(axis)
        forward = [(i, i + 1) for i in range(count - 1)]
        backward = [(target, source) for source, target in forward]
        low = lax.ppermute(
            lax.slice_in_dim(block, block.shape[dim] - width, None, axis=dim), axis, forward
        )
        high = lax.ppermute(lax.slice_in_dim(block, 0, width, axis=dim), axis, backward)
        block = jnp.concatenate([low, block, high], axis=dim)
    return block


def expand(values, factor):
    first, second, third = values.shape
    wide = jnp.broadcast_to(
        values[:, None, :, None, :, None], (first, factor, second, factor, third, factor)
    )
    return wide.reshape(first * factor, second * factor, third * factor)


def mass_along(values, along):
    length = values.shape[along]
    lower = lax.slice_in_dim(values, 0, length - 2, axis=along)
    middle = lax.slice_in_dim(values, 1, length - 1, axis=along)
    upper = lax.slice_in_dim(values, 2, length, axis=along)
    return (lower + 4.0 * middle + upper) / 6.0


def stiff_along(values, along):
    length = values.shape[along]
    lower = lax.slice_in_dim(values, 0, length - 2, axis=along)
    middle = lax.slice_in_dim(values, 1, length - 1, axis=along)
    upper = lax.slice_in_dim(values, 2, length, axis=along)
    return 2.0 * middle - lower - upper


def relax_step(padded, source, inverse, screen):
    padded_all = jnp.pad(padded, ((0, 0), (1, 1), (0, 0)))
    mass_z = mass_along(padded_all, 2)
    stiff_z = stiff_along(padded_all, 2)
    mass_yz = mass_along(mass_z, 1)
    mixed = stiff_along(mass_z, 1) + mass_along(stiff_z, 1)
    laplace = stiff_along(mass_yz, 0) + mass_along(mixed, 0)
    mass_all = mass_along(mass_yz, 0)
    center = padded[1:-1, :, 1:-1]
    return center + relaxation * inverse * (source - laplace - screen * mass_all)


def smooth(field, source, inverse_brick, screen_brick, spread):
    inverse = expand(inverse_brick, spread)
    screen = expand(screen_brick, spread)
    for sweep_index in range(SWEEPS):
        padded = extended(field, (("grp", 0), ("slab", 2)), 1)
        field = relax_step(padded, source, inverse, screen)
    return field


def lift(brick_rows, count_x, count_y, count_z):
    half = BRICK // 2
    cells = brick_rows.reshape(count_x, count_y, count_z, 2, half, 2, half, 2, half)
    pairs = jnp.arange(2, dtype=jnp.int32)
    pick_x = ((jnp.arange(count_x, dtype=jnp.int32) % 2)[:, None] == pairs).astype(jnp.float32)
    pick_y = ((jnp.arange(count_y, dtype=jnp.int32) % 2)[:, None] == pairs).astype(jnp.float32)
    pick_z = ((jnp.arange(count_z, dtype=jnp.int32) % 2)[:, None] == pairs).astype(jnp.float32)
    chosen = jnp.sum(cells * pick_x[:, None, None, :, None, None, None, None, None], axis=3)
    chosen = jnp.sum(chosen * pick_y[None, :, None, None, :, None, None, None], axis=4)
    chosen = jnp.sum(chosen * pick_z[None, None, :, None, None, :, None], axis=5)
    fine = jnp.broadcast_to(
        chosen[:, :, :, :, None, :, None, :, None],
        (count_x, count_y, count_z, half, 2, half, 2, half, 2),
    )
    fine = fine.reshape(count_x, count_y, count_z, BRICK, BRICK, BRICK)
    return fine.transpose(0, 3, 1, 4, 2, 5).reshape(
        count_x * BRICK, count_y * BRICK, count_z * BRICK
    )


def local(source, occupancy, classes, screen_table, parents, coarse):
    shard_len = coarse.shape[1]
    neighbours = extended(coarse, (("slab", 1),), shard_len)
    offset = (lax.axis_index("slab") - 1) * shard_len
    position = (parents - offset).reshape(-1)
    brick_rows = jnp.take(neighbours[0], position, axis=0)
    occupied = occupancy.astype(jnp.float32)
    labels = jnp.arange(screen_table.shape[0], dtype=jnp.int32)
    weight = jnp.sum(jnp.where(classes[..., None] == labels, screen_table, 0.0), axis=-1)
    screen_brick = screen_strength * weight
    inverse_brick = occupied / (stiff_diagonal + screen_brick * mass_diagonal)
    count_x, count_y, count_z = parents.shape
    middle_field = lift(brick_rows, count_x, count_y, count_z) * expand(occupied, BRICK // 2)
    size_x, size_y, size_z = source.shape
    source_mid = 0.25 * source.reshape(size_x // 2, 2, size_y // 2, 2, size_z // 2, 2).sum(
        axis=(1, 3, 5)
    )
    middle_field = smooth(middle_field, source_mid, inverse_brick, screen_brick, BRICK // 2)
    finest_field = expand(middle_field, 2) * expand(occupied, BRICK)
    finest_field = smooth(finest_field, source, inverse_brick, screen_brick, BRICK)
    return (middle_field, finest_field)


def solution(mesh):
    placed = (
        P("grp", None, "slab"),
        P("grp", None, "slab"),
        P("grp", None, "slab"),
        P(),
        P("grp", None, "slab"),
        P("grp", "slab", None),
    )
    return jax.shard_map(
        local,
        mesh=mesh,
        in_specs=placed,
        out_specs=(P("grp", None, "slab"), P("grp", None, "slab")),
        check_vma=False,
    )
```

profile of v0, /device:TPU:13, one launch (start us, length us, event | category | flops | bytes accessed | tf_op | source)
XLA Modules:
  0.0 248.3 jit_solution(15163178675348302549)
XLA Ops:
  0.6 3.8 %collective-permute-start = (f32[1,4,512]{2,1,0:T(4,128)}, f32[1,4,512]{2,1,0:T(4,128)S(1)}, u32[]{:S(2)}, u32[]{:S(2)}) collective-permute-start(f32[1,4,512]{2,1,0:T(4,128)} %param.11), channel_id=1, source_target_pairs={{0,1},{1,2},{2,3},{3,4},{4,5},{5,6},{6,7},{8,9},{9,10},{10,11},{11... | collective-permute-start | bytes 24584 | tf_op jit(solution)/shard_map/ppermute | solution.py:21
  4.4 1.9 collective-permute-start.1
  6.4 0.7 compare_and_fusion
  7.2 0.7 convert_element_type.34
  8.1 1.0 reshape.171
  10.3 0.8 gather.7
  11.2 0.9 multiply_reduce_fusion
  13.9 3.1 %collective-permute-start.2 = (f32[1,16,64]{2,1,0:T(8,128)S(1)}, f32[1,16,64]{2,1,0:T(8,128)S(1)}, u32[]{:S(2)}, u32[]{:S(2)}) collective-permute-start(f32[1,16,64]{2,1,0:T(8,128)S(1)} %get-tuple-element.50), channel_id=1, source_target_pairs={{0,8},{8,16},{16,24},{1,9},{9,17},{17,25},{2,10},{10,18},{18,26},{... | collective-permute-start | bytes 12296 | tf_op jit(solution)/shard_map/ppermute | solution.py:21
  17.0 3.1 %collective-permute-start.3 = (f32[1,16,64]{2,1,0:T(8,128)S(1)}, f32[1,16,64]{2,1,0:T(8,128)S(1)}, u32[]{:S(2)}, u32[]{:S(2)}) collective-permute-start(f32[1,16,64]{2,1,0:T(8,128)S(1)} %get-tuple-element.51), channel_id=1, source_target_pairs={{8,0},{16,8},{24,16},{9,1},{17,9},{25,17},{10,2},{18,10},{26,18},{... | collective-permute-start | bytes 12296 | tf_op jit(solution)/shard_map/ppermute | solution.py:24
  20.3 1.1 collective-permute-done.3
  21.5 4.7 %collective-permute-start.4 = (f32[18,16,1]{2,1,0:T(8,128)S(1)}, f32[18,16,1]{2,1,0:T(8,128)S(1)}, u32[]{:S(2)}, u32[]{:S(2)}) collective-permute-start(f32[18,16,1]{2,1,0:T(8,128)S(1)} %get-tuple-element.44), channel_id=1, source_target_pairs={{0,1},{1,2},{2,3},{3,4},{4,5},{5,6},{6,7},{8,9},{9,10},{10,11},{11... | collective-permute-start | bytes 3464 | tf_op jit(solution)/shard_map/ppermute | solution.py:21
  26.2 1.9 collective-permute-start.5
  28.4 1.0 mul.262
  29.4 1.6 broadcast_in_dim.41
  31.0 2.7 %reshape.173 = f32[16,16,64]{2,1,0:T(8,128)S(1)} reshape(f32[4,4,4,4,16,4]{5,4,3,2,1,0:T(8,128)} %broadcast_in_dim.41) | data formatting | bytes 131072 | tf_op jit(solution)/shard_map/reshape | solution.py:34
  33.8 34.9 %reshape.172 = f32[16,2,16,2,64,2]{5,4,3,2,1,0:T(8,128)} reshape(f32[32,32,128]{2,1,0:T(8,128)S(1)} %copy-done) | data formatting | bytes 1048576 | tf_op jit(solution)/shard_map/reshape | solution.py:108
  68.6 12.2 %reduce_sum.49 = f32[16,16,64]{2,1,0:T(8,128)S(1)} reduce(f32[16,2,16,2,64,2]{5,4,3,2,1,0:T(8,128)} %reshape.172, f32[]{:T(128)} %constant.110.clone.1), dimensions={1,3,5}, to_apply=%region_4.5 | reduce | flops 114688 | bytes 589828 | tf_op jit(solution)/shard_map/reduce_sum | solution.py:108
  81.5 1.9 collective-permute-start.6
  83.4 4.3 %collective-permute-start.7 = (f32[1,16,64]{2,1,0:T(8,128)S(1)}, f32[1,16,64]{2,1,0:T(8,128)S(1)}, u32[]{:S(2)}, u32[]{:S(2)}) collective-permute-start(f32[1,16,64]{2,1,0:T(8,128)S(1)} %get-tuple-element.49), channel_id=1, source_target_pairs={{8,0},{16,8},{24,16},{9,1},{17,9},{25,17},{10,2},{18,10},{26,18},{... | collective-permute-start | bytes 12296 | tf_op jit(solution)/shard_map/ppermute | solution.py:24
  87.7 0.8 collective-permute-done.7
  88.6 4.8 %collective-permute-start.8 = (f32[18,16,1]{2,1,0:T(8,128)S(1)}, f32[18,16,1]{2,1,0:T(8,128)S(1)}, u32[]{:S(2)}, u32[]{:S(2)}) collective-permute-start(f32[18,16,1]{2,1,0:T(8,128)S(1)} %get-tuple-element.42), channel_id=1, source_target_pairs={{0,1},{1,2},{2,3},{3,4},{4,5},{5,6},{6,7},{8,9},{9,10},{10,11},{11... | collective-permute-start | bytes 3464 | tf_op jit(solution)/shard_map/ppermute | solution.py:21
  93.3 1.9 collective-permute-start.9
  95.4 4.4 %collective-permute-done.9 = f32[18,16,1]{2,1,0:T(8,128)S(1)} collective-permute-done((f32[18,16,1]{2,1,0:T(8,128)S(1)}, f32[18,16,1]{2,1,0:T(8,128)S(1)}, u32[]{:S(2)}, u32[]{:S(2)}) %collective-permute-start.9) | collective-permute-done | bytes 1184 | tf_op jit(solution)/shard_map/ppermute | solution.py:24
  100.4 1.9 collective-permute-start.10
  102.3 4.8 %collective-permute-start.11 = (f32[1,16,64]{2,1,0:T(8,128)S(1)}, f32[1,16,64]{2,1,0:T(8,128)S(1)}, u32[]{:S(2)}, u32[]{:S(2)}) collective-permute-start(f32[1,16,64]{2,1,0:T(8,128)S(1)} %get-tuple-element.47), channel_id=1, source_target_pairs={{8,0},{16,8},{24,16},{9,1},{17,9},{25,17},{10,2},{18,10},{26,18},{... | collective-permute-start | bytes 12296 | tf_op jit(solution)/shard_map/ppermute | solution.py:24
  107.2 0.8 collective-permute-done.11
  108.0 2.6 %collective-permute-start.12 = (f32[18,16,1]{2,1,0:T(8,128)S(1)}, f32[18,16,1]{2,1,0:T(8,128)S(1)}, u32[]{:S(2)}, u32[]{:S(2)}) collective-permute-start(f32[18,16,1]{2,1,0:T(8,128)S(1)} %get-tuple-element.40), channel_id=1, source_target_pairs={{0,1},{1,2},{2,3},{3,4},{4,5},{5,6},{6,7},{8,9},{9,10},{10,11},{11... | collective-permute-start | bytes 3464 | tf_op jit(solution)/shard_map/ppermute | solution.py:21
  110.7 2.1 collective-permute-start.13
  112.8 4.1 %broadcast_in_dim.43 = f32[4,8,4,8,16,8]{5,4,3,2,1,0:T(8,128)} broadcast(f32[4,4,16]{2,1,0:T(4,128)S(1)} %convert_element_type.34), dimensions={0,2,4} | broadcast | bytes 525312 | tf_op jit(solution)/shard_map/broadcast_in_dim | solution.py:31
  116.8 6.4 %reshape.175 = f32[32,32,128]{2,1,0:T(8,128)S(1)} reshape(f32[4,8,4,8,16,8]{5,4,3,2,1,0:T(8,128)} %broadcast_in_dim.43) | data formatting | bytes 1048576 | tf_op jit(solution)/shard_map/reshape | solution.py:34
  123.8 11.6 %broadcast_in_dim.42 = f32[16,2,16,2,64,2]{5,4,3,2,1,0:T(8,128)} broadcast(f32[16,16,64]{2,1,0:T(8,128)S(1)} %fusion.46), dimensions={0,2,4} | broadcast | bytes 589824 | tf_op jit(solution)/shard_map/broadcast_in_dim | solution.py:31
  135.4 24.0 %reshape.174 = f32[32,32,128]{2,1,0:T(8,128)S(1)} reshape(f32[16,2,16,2,64,2]{5,4,3,2,1,0:T(8,128)} %broadcast_in_dim.42) | data formatting | bytes 1048576 | tf_op jit(solution)/shard_map/reshape | solution.py:34
  159.5 1.9 collective-permute-start.14
  161.4 4.8 %collective-permute-start.15 = (f32[1,32,128]{2,1,0:T(8,128)S(1)}, f32[1,32,128]{2,1,0:T(8,128)S(1)}, u32[]{:S(2)}, u32[]{:S(2)}) collective-permute-start(f32[1,32,128]{2,1,0:T(8,128)S(1)} %get-tuple-element.27), channel_id=1, source_target_pairs={{8,0},{16,8},{24,16},{9,1},{17,9},{25,17},{10,2},{18,10},{26,18},{... | collective-permute-start | bytes 49160 | tf_op jit(solution)/shard_map/ppermute | solution.py:24
  166.3 0.8 collective-permute-done.15
  167.8 4.5 %collective-permute-start.16 = (f32[34,32,1]{0,1,2:T(8,128)S(1)}, f32[34,32,1]{0,1,2:T(8,128)S(1)}, u32[]{:S(2)}, u32[]{:S(2)}) collective-permute-start(f32[34,32,1]{0,1,2:T(8,128)S(1)} %copy.59), channel_id=1, source_target_pairs={{0,1},{1,2},{2,3},{3,4},{4,5},{5,6},{6,7},{8,9},{9,10},{10,11},{11... | collective-permute-start | bytes 13064 | tf_op jit(solution)/shard_map/ppermute | solution.py:21
  172.7 1.9 collective-permute-start.17
  174.6 4.1 %broadcast_in_dim.44 = f32[4,8,4,8,16,8]{5,4,3,2,1,0:T(8,128)} broadcast(f32[4,4,16]{2,1,0:T(4,128)S(1)} %get-tuple-element.53), dimensions={0,2,4} | broadcast | bytes 525312 | tf_op jit(solution)/shard_map/broadcast_in_dim | solution.py:31
  178.7 6.4 %mul.298 = f32[32,32,128]{2,1,0:T(8,128)S(1)} reshape(f32[4,8,4,8,16,8]{5,4,3,2,1,0:T(8,128)} %broadcast_in_dim.44) | data formatting | bytes 1048576 | tf_op jit(solution)/shard_map/mul | solution.py:62
  185.1 4.1 %broadcast_in_dim.45 = f32[4,8,4,8,16,8]{5,4,3,2,1,0:T(8,128)} broadcast(f32[4,4,16]{2,1,0:T(4,128)S(1)} %get-tuple-element.52), dimensions={0,2,4} | broadcast | bytes 525312 | tf_op jit(solution)/shard_map/broadcast_in_dim | solution.py:31
  189.1 6.4 %reshape.176 = f32[32,32,128]{2,1,0:T(8,128)S(1)} reshape(f32[4,8,4,8,16,8]{5,4,3,2,1,0:T(8,128)} %broadcast_in_dim.45) | data formatting | bytes 1048576 | tf_op jit(solution)/shard_map/reshape | solution.py:34
  196.1 1.3 copy.62
  197.5 1.7 select_maximum_fusion.8
  200.4 1.9 collective-permute-start.18
  202.3 4.8 %collective-permute-start.19 = (f32[1,32,128]{2,1,0:T(8,128)S(1)}, f32[1,32,128]{2,1,0:T(8,128)S(1)}, u32[]{:S(2)}, u32[]{:S(2)}) collective-permute-start(f32[1,32,128]{2,1,0:T(8,128)S(1)} %get-tuple-element.25), channel_id=1, source_target_pairs={{8,0},{16,8},{24,16},{9,1},{17,9},{25,17},{10,2},{18,10},{26,18},{... | collective-permute-start | bytes 49160 | tf_op jit(solution)/shard_map/ppermute | solution.py:24
  207.2 0.8 collective-permute-done.19
  208.1 1.0 fusion.65
  209.1 1.4 copy.63
  210.5 4.7 %collective-permute-start.20 = (f32[34,32,1]{0,1,2:T(8,128)S(1)}, f32[34,32,1]{0,1,2:T(8,128)S(1)}, u32[]{:S(2)}, u32[]{:S(2)}) collective-permute-start(f32[34,32,1]{0,1,2:T(8,128)S(1)} %copy.63), channel_id=1, source_target_pairs={{0,1},{1,2},{2,3},{3,4},{4,5},{5,6},{6,7},{8,9},{9,10},{10,11},{11... | collective-permute-start | bytes 13064 | tf_op jit(solution)/shard_map/ppermute | solution.py:21
  215.6 1.9 collective-permute-start.21
  218.2 2.5 %collective-permute-done.21 = f32[34,32,1]{0,1,2:T(8,128)S(1)} collective-permute-done((f32[34,32,1]{0,1,2:T(8,128)S(1)}, f32[34,32,1]{0,1,2:T(8,128)S(1)}, u32[]{:S(2)}, u32[]{:S(2)}) %collective-permute-start.21) | collective-permute-done | bytes 4384 | tf_op jit(solution)/shard_map/ppermute | solution.py:24
  220.7 1.3 copy.66
  222.0 1.7 select_maximum_fusion.4
  224.9 1.9 collective-permute-start.22
  226.9 4.8 %collective-permute-start.23 = (f32[1,32,128]{2,1,0:T(8,128)S(1)}, f32[1,32,128]{2,1,0:T(8,128)S(1)}, u32[]{:S(2)}, u32[]{:S(2)}) collective-permute-start(f32[1,32,128]{2,1,0:T(8,128)S(1)} %get-tuple-element.23), channel_id=1, source_target_pairs={{8,0},{16,8},{24,16},{9,1},{17,9},{25,17},{10,2},{18,10},{26,18},{... | collective-permute-start | bytes 49160 | tf_op jit(solution)/shard_map/ppermute | solution.py:24
  231.7 0.8 collective-permute-done.23
  232.6 1.0 fusion.64
  233.6 1.4 copy.67
  235.0 2.8 %collective-permute-start.24 = (f32[34,32,1]{0,1,2:T(8,128)S(1)}, f32[34,32,1]{0,1,2:T(8,128)S(1)}, u32[]{:S(2)}, u32[]{:S(2)}) collective-permute-start(f32[34,32,1]{0,1,2:T(8,128)S(1)} %copy.67), channel_id=1, source_target_pairs={{0,1},{1,2},{2,3},{3,4},{4,5},{5,6},{6,7},{8,9},{9,10},{10,11},{11... | collective-permute-start | bytes 13064 | tf_op jit(solution)/shard_map/ppermute | solution.py:21
  238.2 1.9 collective-permute-start.25
  240.8 2.5 %collective-permute-done.25 = f32[34,32,1]{0,1,2:T(8,128)S(1)} collective-permute-done((f32[34,32,1]{0,1,2:T(8,128)S(1)}, f32[34,32,1]{0,1,2:T(8,128)S(1)}, u32[]{:S(2)}, u32[]{:S(2)}) %collective-permute-start.25) | collective-permute-done | bytes 4384 | tf_op jit(solution)/shard_map/ppermute | solution.py:24
  243.3 1.3 copy.70
  244.6 1.7 select_maximum_fusion
  247.1 1.2 fusion.15
  (94 shorter events, 13.0 us)
Async XLA Ops:
  0.6 8.5 %collective-permute-start = (f32[1,4,512]{2,1,0:T(4,128)}, f32[1,4,512]{2,1,0:T(4,128)S(1)}, u32[]{:S(2)}, u32[]{:S(2)}) collective-permute-start(f32[1,4,512]{2,1,0:T(4,128)} %param.11), channel_id=1, source_target_pairs={{0,1},{1,2},{2,3},{3,4},{4,5},{5,6},{6,7},{8,9},{9,10},{10,11},{11... | collective-permute-start | bytes 24584 | tf_op jit(solution)/shard_map/ppermute | solution.py:21
  4.4 5.2 %collective-permute-start.1 = (f32[1,4,512]{2,1,0:T(4,128)}, f32[1,4,512]{2,1,0:T(4,128)S(1)}, u32[]{:S(2)}, u32[]{:S(2)}) collective-permute-start(f32[1,4,512]{2,1,0:T(4,128)} %param.11), channel_id=1, source_target_pairs={{1,0},{2,1},{3,2},{4,3},{5,4},{6,5},{7,6},{9,8},{10,9},{11,10},{12... | collective-permute-start | bytes 24584 | tf_op jit(solution)/shard_map/ppermute | solution.py:24
  8.1 1.5 copy-start.3
  13.2 6.9 %copy-start.4 = (s32[4,4,16]{2,1,0:T(4,128)S(1)}, s32[4,4,16]{2,1,0:T(4,128)}, u32[]{:S(2)}) copy-start(s32[4,4,16]{2,1,0:T(4,128)} %param.8) | copy-start | bytes 3076
  13.2 6.9 %copy-start.5 = (f32[16]{0:T(128)S(1)}, f32[16]{0:T(128)}, u32[]{:S(2)}) copy-start(f32[16]{0:T(128)} %param.9) | copy-start | bytes 196
  13.5 14.6 %copy-start.2 = (s32[4,4,16]{2,1,0:T(4,128)S(1)}, s32[4,4,16]{2,1,0:T(4,128)}, u32[]{:S(2)}) copy-start(s32[4,4,16]{2,1,0:T(4,128)} %param.7) | copy-start | bytes 3076
  13.9 6.4 %collective-permute-start.2 = (f32[1,16,64]{2,1,0:T(8,128)S(1)}, f32[1,16,64]{2,1,0:T(8,128)S(1)}, u32[]{:S(2)}, u32[]{:S(2)}) collective-permute-start(f32[1,16,64]{2,1,0:T(8,128)S(1)} %get-tuple-element.50), channel_id=1, source_target_pairs={{0,8},{8,16},{16,24},{1,9},{9,17},{17,25},{2,10},{10,18},{18,26},{... | collective-permute-start | bytes 12296 | tf_op jit(solution)/shard_map/ppermute | solution.py:21
  17.0 4.4 %collective-permute-start.3 = (f32[1,16,64]{2,1,0:T(8,128)S(1)}, f32[1,16,64]{2,1,0:T(8,128)S(1)}, u32[]{:S(2)}, u32[]{:S(2)}) collective-permute-start(f32[1,16,64]{2,1,0:T(8,128)S(1)} %get-tuple-element.51), channel_id=1, source_target_pairs={{8,0},{16,8},{24,16},{9,1},{17,9},{25,17},{10,2},{18,10},{26,18},{... | collective-permute-start | bytes 12296 | tf_op jit(solution)/shard_map/ppermute | solution.py:24
  21.5 59.3 %collective-permute-start.4 = (f32[18,16,1]{2,1,0:T(8,128)S(1)}, f32[18,16,1]{2,1,0:T(8,128)S(1)}, u32[]{:S(2)}, u32[]{:S(2)}) collective-permute-start(f32[18,16,1]{2,1,0:T(8,128)S(1)} %get-tuple-element.44), channel_id=1, source_target_pairs={{0,1},{1,2},{2,3},{3,4},{4,5},{5,6},{6,7},{8,9},{9,10},{10,11},{11... | collective-permute-start | bytes 3464 | tf_op jit(solution)/shard_map/ppermute | solution.py:21
  26.2 54.6 %collective-permute-start.5 = (f32[18,16,1]{2,1,0:T(8,128)S(1)}, f32[18,16,1]{2,1,0:T(8,128)S(1)}, u32[]{:S(2)}, u32[]{:S(2)}) collective-permute-start(f32[18,16,1]{2,1,0:T(8,128)S(1)} %get-tuple-element.45), channel_id=1, source_target_pairs={{1,0},{2,1},{3,2},{4,3},{5,4},{6,5},{7,6},{9,8},{10,9},{11,10},{12... | collective-permute-start | bytes 3464 | tf_op jit(solution)/shard_map/ppermute | solution.py:24
  31.0 2.7 %copy-start = (f32[32,32,128]{2,1,0:T(8,128)S(1)}, f32[32,32,128]{2,1,0:T(8,128)}, u32[]{:S(2)}) copy-start(f32[32,32,128]{2,1,0:T(8,128)} %param.6) | copy-start | bytes 1572868
  81.5 6.2 %collective-permute-start.6 = (f32[1,16,64]{2,1,0:T(8,128)S(1)}, f32[1,16,64]{2,1,0:T(8,128)S(1)}, u32[]{:S(2)}, u32[]{:S(2)}) collective-permute-start(f32[1,16,64]{2,1,0:T(8,128)S(1)} %get-tuple-element.48), channel_id=1, source_target_pairs={{0,8},{8,16},{16,24},{1,9},{9,17},{17,25},{2,10},{10,18},{18,26},{... | collective-permute-start | bytes 12296 | tf_op jit(solution)/shard_map/ppermute | solution.py:21
  83.4 5.0 %collective-permute-start.7 = (f32[1,16,64]{2,1,0:T(8,128)S(1)}, f32[1,16,64]{2,1,0:T(8,128)S(1)}, u32[]{:S(2)}, u32[]{:S(2)}) collective-permute-start(f32[1,16,64]{2,1,0:T(8,128)S(1)} %get-tuple-element.49), channel_id=1, source_target_pairs={{8,0},{16,8},{24,16},{9,1},{17,9},{25,17},{10,2},{18,10},{26,18},{... | collective-permute-start | bytes 12296 | tf_op jit(solution)/shard_map/ppermute | solution.py:24
  88.6 6.9 %collective-permute-start.8 = (f32[18,16,1]{2,1,0:T(8,128)S(1)}, f32[18,16,1]{2,1,0:T(8,128)S(1)}, u32[]{:S(2)}, u32[]{:S(2)}) collective-permute-start(f32[18,16,1]{2,1,0:T(8,128)S(1)} %get-tuple-element.42), channel_id=1, source_target_pairs={{0,1},{1,2},{2,3},{3,4},{4,5},{5,6},{6,7},{8,9},{9,10},{10,11},{11... | collective-permute-start | bytes 3464 | tf_op jit(solution)/shard_map/ppermute | solution.py:21
  93.3 6.5 %collective-permute-start.9 = (f32[18,16,1]{2,1,0:T(8,128)S(1)}, f32[18,16,1]{2,1,0:T(8,128)S(1)}, u32[]{:S(2)}, u32[]{:S(2)}) collective-permute-start(f32[18,16,1]{2,1,0:T(8,128)S(1)} %get-tuple-element.43), channel_id=1, source_target_pairs={{1,0},{2,1},{3,2},{4,3},{5,4},{6,5},{7,6},{9,8},{10,9},{11,10},{12... | collective-permute-start | bytes 3464 | tf_op jit(solution)/shard_map/ppermute | solution.py:24
  100.4 6.8 %collective-permute-start.10 = (f32[1,16,64]{2,1,0:T(8,128)S(1)}, f32[1,16,64]{2,1,0:T(8,128)S(1)}, u32[]{:S(2)}, u32[]{:S(2)}) collective-permute-start(f32[1,16,64]{2,1,0:T(8,128)S(1)} %get-tuple-element.46), channel_id=1, source_target_pairs={{0,8},{8,16},{16,24},{1,9},{9,17},{17,25},{2,10},{10,18},{18,26},{... | collective-permute-start | bytes 12296 | tf_op jit(solution)/shard_map/ppermute | solution.py:21
  102.3 5.6 %collective-permute-start.11 = (f32[1,16,64]{2,1,0:T(8,128)S(1)}, f32[1,16,64]{2,1,0:T(8,128)S(1)}, u32[]{:S(2)}, u32[]{:S(2)}) collective-permute-start(f32[1,16,64]{2,1,0:T(8,128)S(1)} %get-tuple-element.47), channel_id=1, source_target_pairs={{8,0},{16,8},{24,16},{9,1},{17,9},{25,17},{10,2},{18,10},{26,18},{... | collective-permute-start | bytes 12296 | tf_op jit(solution)/shard_map/ppermute | solution.py:24
  108.0 15.2 %collective-permute-start.12 = (f32[18,16,1]{2,1,0:T(8,128)S(1)}, f32[18,16,1]{2,1,0:T(8,128)S(1)}, u32[]{:S(2)}, u32[]{:S(2)}) collective-permute-start(f32[18,16,1]{2,1,0:T(8,128)S(1)} %get-tuple-element.40), channel_id=1, source_target_pairs={{0,1},{1,2},{2,3},{3,4},{4,5},{5,6},{6,7},{8,9},{9,10},{10,11},{11... | collective-permute-start | bytes 3464 | tf_op jit(solution)/shard_map/ppermute | solution.py:21
  110.7 12.6 %collective-permute-start.13 = (f32[18,16,1]{2,1,0:T(8,128)S(1)}, f32[18,16,1]{2,1,0:T(8,128)S(1)}, u32[]{:S(2)}, u32[]{:S(2)}) collective-permute-start(f32[18,16,1]{2,1,0:T(8,128)S(1)} %get-tuple-element.41), channel_id=1, source_target_pairs={{1,0},{2,1},{3,2},{4,3},{5,4},{6,5},{7,6},{9,8},{10,9},{11,10},{12... | collective-permute-start | bytes 3464 | tf_op jit(solution)/shard_map/ppermute | solution.py:24
  123.8 11.6 %copy-start.1 = (f32[16,16,64]{2,1,0:T(8,128)}, f32[16,16,64]{2,1,0:T(8,128)S(1)}, u32[]{:S(2)}) copy-start(f32[16,16,64]{2,1,0:T(8,128)S(1)} %fusion.46) | copy-start | bytes 196612
  159.5 6.8 %collective-permute-start.14 = (f32[1,32,128]{2,1,0:T(8,128)S(1)}, f32[1,32,128]{2,1,0:T(8,128)S(1)}, u32[]{:S(2)}, u32[]{:S(2)}) collective-permute-start(f32[1,32,128]{2,1,0:T(8,128)S(1)} %get-tuple-element.26), channel_id=1, source_target_pairs={{0,8},{8,16},{16,24},{1,9},{9,17},{17,25},{2,10},{10,18},{18,26},{... | collective-permute-start | bytes 49160 | tf_op jit(solution)/shard_map/ppermute | solution.py:21
  161.4 5.7 %collective-permute-start.15 = (f32[1,32,128]{2,1,0:T(8,128)S(1)}, f32[1,32,128]{2,1,0:T(8,128)S(1)}, u32[]{:S(2)}, u32[]{:S(2)}) collective-permute-start(f32[1,32,128]{2,1,0:T(8,128)S(1)} %get-tuple-element.27), channel_id=1, source_target_pairs={{8,0},{16,8},{24,16},{9,1},{17,9},{25,17},{10,2},{18,10},{26,18},{... | collective-permute-start | bytes 49160 | tf_op jit(solution)/shard_map/ppermute | solution.py:24
  167.8 27.7 %collective-permute-start.16 = (f32[34,32,1]{0,1,2:T(8,128)S(1)}, f32[34,32,1]{0,1,2:T(8,128)S(1)}, u32[]{:S(2)}, u32[]{:S(2)}) collective-permute-start(f32[34,32,1]{0,1,2:T(8,128)S(1)} %copy.59), channel_id=1, source_target_pairs={{0,1},{1,2},{2,3},{3,4},{4,5},{5,6},{6,7},{8,9},{9,10},{10,11},{11... | collective-permute-start | bytes 13064 | tf_op jit(solution)/shard_map/ppermute | solution.py:21
  172.7 23.4 %collective-permute-start.17 = (f32[34,32,1]{0,1,2:T(8,128)S(1)}, f32[34,32,1]{0,1,2:T(8,128)S(1)}, u32[]{:S(2)}, u32[]{:S(2)}) collective-permute-start(f32[34,32,1]{0,1,2:T(8,128)S(1)} %copy.60), channel_id=1, source_target_pairs={{1,0},{2,1},{3,2},{4,3},{5,4},{6,5},{7,6},{9,8},{10,9},{11,10},{12... | collective-permute-start | bytes 13064 | tf_op jit(solution)/shard_map/ppermute | solution.py:24
  200.4 6.8 %collective-permute-start.18 = (f32[1,32,128]{2,1,0:T(8,128)S(1)}, f32[1,32,128]{2,1,0:T(8,128)S(1)}, u32[]{:S(2)}, u32[]{:S(2)}) collective-permute-start(f32[1,32,128]{2,1,0:T(8,128)S(1)} %get-tuple-element.24), channel_id=1, source_target_pairs={{0,8},{8,16},{16,24},{1,9},{9,17},{17,25},{2,10},{10,18},{18,26},{... | collective-permute-start | bytes 49160 | tf_op jit(solution)/shard_map/ppermute | solution.py:21
  202.3 5.7 %collective-permute-start.19 = (f32[1,32,128]{2,1,0:T(8,128)S(1)}, f32[1,32,128]{2,1,0:T(8,128)S(1)}, u32[]{:S(2)}, u32[]{:S(2)}) collective-permute-start(f32[1,32,128]{2,1,0:T(8,128)S(1)} %get-tuple-element.25), channel_id=1, source_target_pairs={{8,0},{16,8},{24,16},{9,1},{17,9},{25,17},{10,2},{18,10},{26,18},{... | collective-permute-start | bytes 49160 | tf_op jit(solution)/shard_map/ppermute | solution.py:24
  210.5 7.1 %collective-permute-start.20 = (f32[34,32,1]{0,1,2:T(8,128)S(1)}, f32[34,32,1]{0,1,2:T(8,128)S(1)}, u32[]{:S(2)}, u32[]{:S(2)}) collective-permute-start(f32[34,32,1]{0,1,2:T(8,128)S(1)} %copy.63), channel_id=1, source_target_pairs={{0,1},{1,2},{2,3},{3,4},{4,5},{5,6},{6,7},{8,9},{9,10},{10,11},{11... | collective-permute-start | bytes 13064 | tf_op jit(solution)/shard_map/ppermute | solution.py:21
  215.6 5.0 %collective-permute-start.21 = (f32[34,32,1]{0,1,2:T(8,128)S(1)}, f32[34,32,1]{0,1,2:T(8,128)S(1)}, u32[]{:S(2)}, u32[]{:S(2)}) collective-permute-start(f32[34,32,1]{0,1,2:T(8,128)S(1)} %copy.64), channel_id=1, source_target_pairs={{1,0},{2,1},{3,2},{4,3},{5,4},{6,5},{7,6},{9,8},{10,9},{11,10},{12... | collective-permute-start | bytes 13064 | tf_op jit(solution)/shard_map/ppermute | solution.py:24
  224.9 6.8 %collective-permute-start.22 = (f32[1,32,128]{2,1,0:T(8,128)S(1)}, f32[1,32,128]{2,1,0:T(8,128)S(1)}, u32[]{:S(2)}, u32[]{:S(2)}) collective-permute-start(f32[1,32,128]{2,1,0:T(8,128)S(1)} %get-tuple-element.22), channel_id=1, source_target_pairs={{0,8},{8,16},{16,24},{1,9},{9,17},{17,25},{2,10},{10,18},{18,26},{... | collective-permute-start | bytes 49160 | tf_op jit(solution)/shard_map/ppermute | solution.py:21
  226.9 5.7 %collective-permute-start.23 = (f32[1,32,128]{2,1,0:T(8,128)S(1)}, f32[1,32,128]{2,1,0:T(8,128)S(1)}, u32[]{:S(2)}, u32[]{:S(2)}) collective-permute-start(f32[1,32,128]{2,1,0:T(8,128)S(1)} %get-tuple-element.23), channel_id=1, source_target_pairs={{8,0},{16,8},{24,16},{9,1},{17,9},{25,17},{10,2},{18,10},{26,18},{... | collective-permute-start | bytes 49160 | tf_op jit(solution)/shard_map/ppermute | solution.py:24
  235.0 5.1 %collective-permute-start.24 = (f32[34,32,1]{0,1,2:T(8,128)S(1)}, f32[34,32,1]{0,1,2:T(8,128)S(1)}, u32[]{:S(2)}, u32[]{:S(2)}) collective-permute-start(f32[34,32,1]{0,1,2:T(8,128)S(1)} %copy.67), channel_id=1, source_target_pairs={{0,1},{1,2},{2,3},{3,4},{4,5},{5,6},{6,7},{8,9},{9,10},{10,11},{11... | collective-permute-start | bytes 13064 | tf_op jit(solution)/shard_map/ppermute | solution.py:21
  238.2 5.0 %collective-permute-start.25 = (f32[34,32,1]{0,1,2:T(8,128)S(1)}, f32[34,32,1]{0,1,2:T(8,128)S(1)}, u32[]{:S(2)}, u32[]{:S(2)}) collective-permute-start(f32[34,32,1]{0,1,2:T(8,128)S(1)} %copy.68), channel_id=1, source_target_pairs={{1,0},{2,1},{3,2},{4,3},{5,4},{6,5},{7,6},{9,8},{10,9},{11,10},{12... | collective-permute-start | bytes 13064 | tf_op jit(solution)/shard_map/ppermute | solution.py:24
where the time goes:
time: 253 us; the launch traced here: 248 us
  local copies, waits for them, and re-layouts  124 us (49%)
  starting transfers between devices  80.7 us (32%)
  other arithmetic  26.8 us (11%)
  waiting for transfers between devices  15.1 us (6%)
    ppermute x13, starting transfers between devices, extended(): lax.ppermute(lax.slice_in_dim(block, block.shape[dim] - width, None, axis...  40.5 us
    reshape x5, local copies, waits for them, and re-layouts, expand(): return wide.reshape(first * factor, second * factor, third * factor)  40.5 us
    ppermute x13, starting transfers between devices, extended(): lax.ppermute(lax.slice_in_dim(block, 0, width, axis=dim), axis, backward)  40.2 us
    reshape x1, local copies, waits for them, and re-layouts, local(): source.reshape(size_x // 2, 2, size_y // 2, 2, size_z // 2, 2)  34.9 us
    broadcast_in_dim x7, local copies, waits for them, and re-layouts, expand(): jnp.broadcast_to(values[:, None, :, None, :, None], (first, factor, secon...  25.8 us
    ppermute x13, waiting for transfers between devices, extended(): lax.ppermute(lax.slice_in_dim(block, 0, width, axis=dim), axis, backward)  15 us
    reduce_sum x1, other arithmetic, local(): source.reshape(size_x // 2, 2, size_y // 2, 2, size_z // 2, 2)  12.2 us
    mul x2, local copies, waits for them, and re-layouts, relax_step(): relaxation * inverse * (source - laplace - screen * mass_all)  7.4 us
  transfers between devices with their start and end apart: 26, of which 11 were waited for; matrix products, arithmetic and copies ran while one was open for 36% of the time, Pallas kernels for 0%

commit v1 on v0

v1 whole, which is shorter than its diff:
```python
import functools
import jax
import jax.numpy as jnp
import numpy as np
from jax import lax
from jax.experimental import pallas as pl
from jax.experimental.pallas import tpu as pltpu
from jax.sharding import PartitionSpec as P

BRICK = 8
F32 = jnp.float32
BF16 = jnp.bfloat16
MESH = pl.DeviceIdType.MESH
VM = pl.BlockSpec(memory_space=pltpu.VMEM)
SM = pl.BlockSpec(memory_space=pltpu.SMEM)

NEAR = [(dx, dz) for dx in (-1, 0, 1) for dz in (-2, -1, 0, 1, 2) if (dx, dz) != (0, 0)]


def split3(a):
    hi = a.astype(BF16)
    rest = a - hi.astype(F32)
    mid = rest.astype(BF16)
    lo = (rest - mid.astype(F32)).astype(BF16)
    return hi, mid, lo


def dot3(a, b):
    parts = [jnp.dot(p, b, preferred_element_type=F32) for p in split3(a)]
    return parts[0] + (parts[1] + parts[2])


def iota(shape, dim):
    return lax.broadcasted_iota(jnp.int32, shape, dim)


def exchange_kernel(
    groups, slabs, source, occ, cls, par, coarse, fold,
    msgz, s13, rz, rc, rf, rfx, rsrc, rs13,
    msgx, xs13, send_sem, recv_sem,
):
    g = lax.axis_index("grp")
    s = lax.axis_index("slab")
    nx, ny, nz = source.shape
    half = nx // 2

    def exists(dx, dz):
        return (g + dx >= 0) & (g + dx < groups) & (s + dz >= 0) & (s + dz < slabs)

    for ref in (rz, rc, rf, rfx, rsrc, rs13):
        ref[...] = jnp.zeros(ref.shape, F32)
    barrier = pltpu.get_barrier_semaphore()
    count = jnp.int32(0)
    for dx, dz in NEAR:
        here = exists(dx, dz)
        count = count + here.astype(jnp.int32)

        @pl.when(here)
        def _():
            pl.semaphore_signal(
                barrier, inc=1, device_id={"grp": g + dx, "slab": s + dz}, device_id_type=MESH
            )

    lane = iota((8, 128), 1)
    for c in range(4):
        msgz[4 * c : 4 * c + 4, :] = coarse[0, :, 128 * c : 128 * c + 128]
    msgz[16:32, :] = jnp.zeros((16, 128), F32)
    bx = occ.shape[0]
    for i in range(bx):
        msgz[16 + 4 * i : 20 + 4 * i, 0:16] = occ[i].astype(F32)
        msgz[16 + 4 * i : 20 + 4 * i, 16:32] = cls[i].astype(F32)
    msgz[16:32, 32:40] = jnp.broadcast_to(par[0, 0:1, :].astype(F32), (16, 8))
    for t in range(4):
        tile = jnp.zeros((8, 128), F32)
        for j in range(8):
            for yh in range(4):
                off = (j * 4 + yh) * 4
                v = source[t * 8 + j, yh * 8 : yh * 8 + 8, :]
                r = pltpu.roll(v, off, 1) if off else v
                tile = jnp.where(((lane + 2 - off) & 127) < 4, r, tile)
        msgz[32 + 8 * t : 40 + 8 * t, :] = tile
    for m in range(half):
        a = source[2 * m, pl.ds(0, 16, 2), :] + source[2 * m, pl.ds(1, 16, 2), :]
        b = source[2 * m + 1, pl.ds(0, 16, 2), :] + source[2 * m + 1, pl.ds(1, 16, 2), :]
        s13[m] = a + b
    flat = s13[...].reshape(half * 16, 128)
    s13[...] = dot3(flat, fold[...]).reshape(half, 16, 128)
    for t in range(2):
        tile = jnp.zeros((8, 128), F32)
        for j in range(8):
            for yh in range(2):
                off = (j * 2 + yh) * 8
                v = s13[t * 8 + j, yh * 8 : yh * 8 + 8, :]
                low = pltpu.roll(v, (off + 4) % 128, 1)
                high = pltpu.roll(v, (off + 68) % 128, 1)
                tile = jnp.where((lane >= off) & (lane < off + 4), high, tile)
                tile = jnp.where((lane >= off + 4) & (lane < off + 8), low, tile)
        msgz[64 + 8 * t : 72 + 8 * t, :] = tile
    lane16 = iota((16, 128), 1)
    for side in range(2):
        msgx[side, 0:8, :] = msgz[8 * side : 8 * side + 8, :]
        msgx[side, 8:16, :] = msgz[16 + 8 * side : 24 + 8 * side, :]
        msgx[side, 16:24, :] = msgz[32 + 24 * side : 40 + 24 * side, :]
        msgx[side, 24:32, :] = msgz[64 + 8 * side : 72 + 8 * side, :]
        base = (half - 4) * side
        for i in range(2):
            xs13[side, i] = jnp.where(
                lane16 < 64, s13[base + i], pltpu.roll(s13[base + 2 + i], 64, 1)
            )

    pl.semaphore_wait(barrier, count)

    copies = []

    def add(src, dst, dx, dz):
        k = len(copies)
        copies.append((src, dst, dx, dz, k))

    for dz in (-1, 1):
        add(msgz, rz.at[(1 - dz) // 2], 0, dz)
    for dx in (-1, 1):
        side, slot = (dx + 1) // 2, (1 - dx) // 2
        add(source.at[(nx - 2) * side : (nx - 2) * side + 2], rsrc.at[slot], dx, 0)
        add(xs13.at[side], rs13.at[slot], dx, 0)
        add(msgx.at[side, 0:16], rc.at[slot, 1, 0:16], dx, 0)
        for dz in (-1, 1):
            add(msgx.at[side], rc.at[slot, 1 - dz], dx, dz)
        for dz in (-2, 2):
            add(msgx.at[side, 0:8], rfx.at[slot, (2 - dz) // 4], dx, dz)
    for dz in (-2, 2):
        add(msgz.at[0:16], rf.at[(2 - dz) // 4], 0, dz)

    made = []
    for src, dst, dx, dz, k in copies:
        copy = pltpu.make_async_remote_copy(
            src_ref=src, dst_ref=dst, send_sem=send_sem.at[k], recv_sem=recv_sem.at[k],
            device_id={"grp": g + dx, "slab": s + dz}, device_id_type=MESH,
        )
        made.append((copy, dx, dz))
        pl.when(exists(dx, dz))(copy.start)
    for copy, dx, dz in made:
        pl.when(exists(-dx, -dz))(copy.wait_recv)
    for copy, dx, dz in made:
        pl.when(exists(dx, dz))(copy.wait_send)


def y_sum(v):
    rows = v.shape[0]
    at = iota(v.shape, 0)
    up = jnp.where(at == 0, 0.0, pltpu.roll(v, 1, 0))
    down = jnp.where(at == rows - 1, 0.0, pltpu.roll(v, rows - 1, 0))
    return up + down


def parts_of(v, zs):
    b = 4.0 * v + zs
    a = 4.0 * v + y_sum(v)
    c = 4.0 * b + y_sum(b)
    return c, a + b


def smooth_kernel(
    slab_rows, table, source, msgz, s13, rz, rc, rf, rfx, rsrc, rs13, fc, fd, fe,
    middle, finest,
    pf, px, qx, pm, qm, occm, occf, v13, wr13, v14, wr14,
):
    s = lax.axis_index("slab")
    nx, ny, nz = source.shape
    half = nx // 2

    def ext(own, low, high):
        lane = iota(own.shape, 1)
        return jnp.where(
            lane < 40, own, jnp.where(lane < 80, pltpu.roll(low, 40, 1), pltpu.roll(high, 80, 1))
        )

    e_low = ext(rc[0, 1, 8:16], rc[0, 0, 8:16], rc[0, 2, 8:16])
    e_own = ext(msgz[16:32], rz[0, 16:32], rz[1, 16:32])
    e_high = ext(rc[1, 1, 8:16], rc[1, 0, 8:16], rc[1, 2, 8:16])
    e_all = jnp.concatenate([e_low, e_own, e_high], axis=0)
    spread = jnp.dot(e_all.astype(BF16), fc[...], preferred_element_type=F32)

    def coefficients(occupied, label):
        weight = jnp.zeros_like(label)
        for i in range(table.shape[0]):
            weight = jnp.where(label == float(i), table[i], weight)
        screen = 4.0 * weight
        inverse = occupied / (8.0 / 3.0 + screen * (8.0 / 27.0))
        p = inverse * (1.0 / 9.0)
        return p, p * ((screen - 18.0) * (1.0 / 36.0))

    of, om = spread[:, 0:256], spread[:, 512:640]
    p, q = coefficients(of, spread[:, 256:512])
    pf[...] = p
    for i in range(8):
        for j in range(4):
            for tile in range(2):
                cut = slice(128 * tile, 128 * tile + 128)
                one = slice(4 * i + j, 4 * i + j + 1)
                px[i, tile, 8 * j : 8 * j + 8, :] = jnp.broadcast_to(p[one, cut], (8, 128))
                qx[i, tile, 8 * j : 8 * j + 8, :] = jnp.broadcast_to(q[one, cut], (8, 128))
    p, q = coefficients(om, spread[:, 640:768])
    for i in range(8):
        for value, ref in ((p, pm), (q, qm), (om, occm), (of, occf)):
            rows = [
                jnp.broadcast_to(value[4 * i + j : 4 * i + j + 1], (4, value.shape[1]))
                for j in range(4)
            ]
            ref[i] = jnp.concatenate(rows, axis=0)

    base = ((s - 2) * slab_rows).astype(F32)

    def bricks(ext_rows, blocks, cs):
        cand = jnp.concatenate(blocks, axis=0)
        n_rows, n_cand = cs * 8, 5 * cs * 4
        row = jnp.broadcast_to(ext_rows[0:1], (n_rows, 128))
        kk = iota((n_rows, 128), 0) & 7
        at = jnp.where(kk == 0, 78, jnp.where(kk == 5, 112, 30 + 2 * kk))
        at = jnp.where(kk > 5, 127, at)
        pos = jnp.sum(jnp.where(iota((n_rows, 128), 1) == at, row, 0.0), axis=1, keepdims=True)
        col = iota((n_rows, n_cand), 1)
        r = iota((n_rows, n_cand), 0)
        block = col // (cs * 4)
        c_of = (col // 4) % cs
        place = (block * 4 + col % 4).astype(F32)
        hot = ((c_of == r // 8) & (pos - base == place)).astype(F32).astype(BF16)
        hi, mid, lo = split3(cand)
        return [jnp.dot(hot, part, preferred_element_type=F32) for part in (hi, mid, lo)]

    own = bricks(e_own, [rf[0], rz[0, 0:16], msgz[0:16], rz[1, 0:16], rf[1]], 4)
    sides = [
        bricks(e, [rfx[i, 0], rc[i, 0, 0:8], rc[i, 1, 0:8], rc[i, 2, 0:8], rfx[i, 1]], 2)
        for i, e in ((0, e_low), (1, e_high))
    ]
    keep = (iota((16, 128), 1) // 8) == iota((16, 128), 0)
    total = None
    for part in range(3):
        lines = []
        for rows, cs in ((sides[0][part], 2), (own[part], 4), (sides[1][part], 2)):
            for c in range(cs):
                lines.append(jnp.concatenate(
                    [
                        jnp.where(keep, jnp.broadcast_to(rows[8 * c + k : 8 * c + k + 1], (16, 128)), 0.0)
                        for k in range(6)
                    ], axis=1))
        left = jnp.concatenate(lines, axis=0).astype(BF16)
        term = jnp.dot(left, fd[...], preferred_element_type=F32)
        total = term if total is None else total + term
    for i in range(1, 15):
        line = total[8 * i : 8 * i + 8]
        for a in range(2):
            plane = 2 * i - 2 + a
            v13[0, plane, pl.ds(0, 8, 2), :] = line
            v13[0, plane, pl.ds(1, 8, 2), :] = line
    for plane in range(28):
        brick = min(max((plane - 6) // 4 + 2, 0), 7)
        v13[0, plane] = v13[0, plane] * occm[brick]

    lane16 = iota((16, 128), 1)
    lane8 = iota((8, 128), 1)

    def strip13(low, high, j, own_plane):
        both = jnp.where((lane8 & 7) < 4, low, high)
        rows = []
        for yh in range(2):
            off = (j * 2 + yh) * 8
            to_low = pltpu.roll(both, (124 - off) % 128, 1)
            to_high = pltpu.roll(both, (60 - off) % 128, 1)
            rows.append(jnp.where(
                lane8 < 64, own_plane[8 * yh : 8 * yh + 8],
                jnp.where(lane8 < 96, to_high, to_low)))
        return jnp.concatenate(rows, axis=0)

    for m in range(-4, half + 4):
        if m < 0 or m >= half:
            side, i = (0, m + 4) if m < 0 else (1, m - half)
            own_plane = rs13[side, i % 2]
            if i >= 2:
                own_plane = pltpu.roll(own_plane, 64, 1)
            j = (m if m >= 0 else half + m) % 8
            plane = strip13(rc[side, 0, 24:32], rc[side, 2, 24:32], j, own_plane)
        else:
            t = m // 8
            plane = strip13(rz[0, 64 + 8 * t : 72 + 8 * t], rz[1, 64 + 8 * t : 72 + 8 * t], m % 8, s13[m])
        wr13[m + 4] = plane * (6.0 * pm[m // 4 + 2])

    def strip14(low, high, j):
        both = jnp.where((lane8 & 3) < 2, high, low)
        rows = []
        for yh in range(4):
            off = (j * 4 + yh) * 4
            rows.append(pltpu.roll(both, 128 - off, 1) if off else both)
        return rows

    for x in range(-2, nx + 2):
        if x < 0 or x >= nx:
            side, i = (0, x + 2) if x < 0 else (1, x - nx)
            own_plane = rsrc[side, i]
            j = (x if x >= 0 else nx + x) % 8
            rows = strip14(rc[side, 0, 16:24], rc[side, 2, 16:24], j)
        else:
            t = x // 8
            own_plane = source[x]
            rows = strip14(rz[0, 32 + 8 * t : 40 + 8 * t], rz[1, 32 + 8 * t : 40 + 8 * t], x % 8)
        xb = x // 8 + 2
        for yh in range(4):
            w = 6.0 * pf[4 * xb + yh : 4 * xb + yh + 1, :]
            wr14[x + 2, 8 * yh : 8 * yh + 8, 0:128] = own_plane[8 * yh : 8 * yh + 8] * w[:, 0:128]
            wr14[x + 2, 8 * yh : 8 * yh + 8, 128:256] = rows[yh] * w[:, 128:256]

    for sweep in range(3):
        old, new = sweep % 2, (sweep + 1) % 2
        first, last = sweep - 4, half + 3 - sweep

        def pieces(i):
            v = v13[old, i + 6]
            return parts_of(v, pltpu.roll(v, 1, 1) + pltpu.roll(v, 127, 1))

        c0, e0 = pieces(first - 1)
        c1, e1 = pieces(first)
        for m in range(first, last + 1):
            c2, e2 = pieces(m + 1)
            b = m // 4 + 2
            bx_e = 4.0 * e1 + (e0 + e2)
            bx_c = 4.0 * c1 + (c0 + c2)
            out = v13[old, m + 6] + wr13[m + 4] - pm[b] * (c1 + bx_e) - qm[b] * bx_c
            v13[new, m + 6] = out
            if sweep == 2 and 0 <= m < half:
                middle[m] = out[:, 0:64]
            c0, e0, c1, e1 = c1, e1, c2, e2

    wide = dot3(v13[1, 4 : half + 8].reshape((half + 4) * 16, 128), fe[...])
    for i in range(half + 4):
        m = i - 2
        line = wide[16 * i : 16 * i + 16] * occf[m // 4 + 2]
        for a in range(2):
            for b in range(2):
                v14[0, 2 * i + a, b, pl.ds(0, 16, 2), :] = line[:, 128 * b : 128 * b + 128]
                v14[0, 2 * i + a, b, pl.ds(1, 16, 2), :] = line[:, 128 * b : 128 * b + 128]

    lane32 = iota((ny, 128), 1)
    for sweep in range(3):
        old, new = sweep % 2, (sweep + 1) % 2
        first, last = sweep - 2, nx + 1 - sweep
        tiles = 2 if sweep < 2 else 1

        def pieces(i):
            v0 = v14[old, i, 0]
            v1 = v14[old, i, 1]
            l0, l1 = pltpu.roll(v0, 1, 1), pltpu.roll(v1, 1, 1)
            r0, r1 = pltpu.roll(v0, 127, 1), pltpu.roll(v1, 127, 1)
            z0 = jnp.where(lane32 == 0, l1, l0) + jnp.where(lane32 == 127, r1, r0)
            got = [parts_of(v0, z0)]
            if tiles == 2:
                z1 = jnp.where(lane32 == 0, l0, l1) + jnp.where(lane32 == 127, r0, r1)
                got.append(parts_of(v1, z1))
            return got

        def step(i, carry):
            before, now = carry
            after = pieces(i + 1)
            xb = (i + 12) // 8
            for t in range(tiles):
                cut = slice(128 * t, 128 * t + 128)
                (c0, e0), (c1, e1), (c2, e2) = before[t], now[t], after[t]
                u = c1 + (4.0 * e1 + (e0 + e2))
                w = 4.0 * c1 + (c0 + c2)
                for yh in range(4):
                    r = slice(8 * yh, 8 * yh + 8)
                    p = px[xb, t, r]
                    q = qx[xb, t, r]
                    out = v14[old, i, t, r] + wr14[i - 2, r, cut] - p * u[r] - q * w[r]
                    if sweep == 2:
                        finest[i - 4, r, :] = out
                    else:
                        v14[new, i, t, r] = out
            return now, after

        lax.fori_loop(first + 4, last + 5, step, (pieces(first + 3), pieces(first + 4)))


def constants():
    fc = np.zeros((128, 768), np.float32)
    for j in range(256):
        z = j if j < 192 else j - 256
        if 0 <= z < 128:
            at = z // 8
        elif -16 <= z < 0:
            at = 56 + z // 8
        elif 128 <= z < 144:
            at = 80 + (z - 128) // 8
        else:
            continue
        fc[at, j] = 1
        fc[at + 16, 256 + j] = 1
    for j in range(128):
        z = j if j < 96 else j - 128
        if 0 <= z < 64:
            at = z // 4
        elif -8 <= z < 0:
            at = 56 + z // 4
        elif 64 <= z < 72:
            at = 80 + (z - 64) // 4
        else:
            continue
        fc[at, 512 + j] = 1
        fc[at + 16, 640 + j] = 1
    fd = np.zeros((768, 128), np.float32)
    for k in range(6):
        for l in range(128):
            for b in range(2):
                z = (k - 1) * 16 + 2 * (l % 8) + b
                if -8 <= z < 72:
                    fd[k * 128 + l, z % 128] = 1
    fe = np.zeros((128, 256), np.float32)
    for j in range(256):
        z = j if j < 192 else j - 256
        if -8 <= z < 136:
            fe[(z // 2) % 128, j] = 1
    fold = np.zeros((128, 128), np.float32)
    for z in range(128):
        fold[z, z // 2] = 0.25
    return [jnp.asarray(a, BF16) for a in (fold, fc, fd, fe)]


def local(groups, slabs, source, occupancy, classes, screen_table, parents, coarse):
    nx, ny, nz = source.shape
    half = nx // 2
    fold, fc, fd, fe = constants()
    shape = lambda *dims: jax.ShapeDtypeStruct(dims, F32)
    moved = pl.pallas_call(
        functools.partial(exchange_kernel, groups, slabs),
        out_shape=[
            shape(80, 128), shape(half, 16, 128), shape(2, 80, 128), shape(2, 3, 32, 128),
            shape(2, 16, 128), shape(2, 2, 8, 128), shape(2, 2, ny, nz), shape(2, 2, 16, 128),
        ],
        in_specs=[VM] * 6,
        out_specs=[VM] * 8,
        scratch_shapes=[
            pltpu.VMEM((2, 32, 128), F32),
            pltpu.VMEM((2, 2, 16, 128), F32),
            pltpu.SemaphoreType.DMA((18,)),
            pltpu.SemaphoreType.DMA((18,)),
        ],
        compiler_params=pltpu.CompilerParams(
            collective_id=0, has_side_effects=True, vmem_limit_bytes=24 << 20
        ),
        name="exchange",
    )(source, occupancy, classes, parents, coarse, fold)
    return pl.pallas_call(
        functools.partial(smooth_kernel, coarse.shape[1]),
        out_shape=[shape(half, ny // 2, nz // 2), shape(nx, ny, nz)],
        in_specs=[SM] + [VM] * 12,
        out_specs=[VM] * 2,
        scratch_shapes=[
            pltpu.VMEM((32, 256), F32),
            pltpu.VMEM((8, 2, ny, 128), F32), pltpu.VMEM((8, 2, ny, 128), F32),
            pltpu.VMEM((8, 16, 128), F32), pltpu.VMEM((8, 16, 128), F32),
            pltpu.VMEM((8, 16, 128), F32), pltpu.VMEM((8, 16, 256), F32),
            pltpu.VMEM((2, half + 12, 16, 128), F32),
            pltpu.VMEM((half + 8, 16, 128), F32),
            pltpu.VMEM((2, nx + 8, 2, ny, 128), F32),
            pltpu.VMEM((nx + 4, ny, 256), F32),
        ],
        compiler_params=pltpu.CompilerParams(vmem_limit_bytes=32 << 20),
        name="smooth",
    )(screen_table, source, *moved, fc, fd, fe)


def solution(mesh):
    placed = (
        P("grp", None, "slab"),
        P("grp", None, "slab"),
        P("grp", None, "slab"),
        P(),
        P("grp", None, "slab"),
        P("grp", "slab", None),
    )
    return jax.shard_map(
        functools.partial(local, mesh.shape["grp"], mesh.shape["slab"]),
        mesh=mesh,
        in_specs=placed,
        out_specs=(P("grp", None, "slab"), P("grp", None, "slab")),
        check_vma=False,
    )
```

time: 253 us -> 31.4 us (0.12); the launches traced: 248 us -> 30.9 us
  local copies, waits for them, and re-layouts: 124 us -> 7.05 us
  starting transfers between devices: 80.7 us -> 0 us
  other arithmetic: 26.8 us -> 0 us
  Pallas kernels: 0 us -> 23.2 us
  waiting for transfers between devices: 15.1 us -> 0 us
    ppermute x26 -> x0, starting transfers between devices: 80.7 us -> none  [the longest x13 40.5 us: extended(): lax.ppermute(lax.slice_in_dim(block, block.shape[dim] - width, None, axis...]
    reshape x8 -> x0, local copies, waits for them, and re-layouts: 75.8 us -> none  [the longest x5 40.5 us: expand(): return wide.reshape(first * factor, second * factor, third * factor)]
    broadcast_in_dim x8 -> x0, local copies, waits for them, and re-layouts: 26.1 us -> none  [the longest x7 25.8 us: expand(): jnp.broadcast_to(values[:, None, :, None, :, None], (first, factor, secon...]
    pallas_call x0 -> x2, Pallas kernels: none -> 23.2 us  [the longest x1 13.6 us: local(): pl.pallas_call(functools.partial(smooth_kernel, coarse.shape[1]), out_sha...]
    ppermute x26 -> x0, waiting for transfers between devices: 15.1 us -> none  [the longest x13 15 us: extended(): lax.ppermute(lax.slice_in_dim(block, 0, width, axis=dim), axis, backward)]
    reduce_sum x5 -> x0, other arithmetic: 14 us -> none  [the longest x1 12.2 us: local(): source.reshape(size_x // 2, 2, size_y // 2, 2, size_z // 2, 2)]
    mul x2 -> x0, local copies, waits for them, and re-layouts: 7.4 us -> none  [relax_step(): relaxation * inverse * (source - laplace - screen * mass_all)]
    slice x18 -> x0, local copies, waits for them, and re-layouts: 7.09 us -> none  [the longest x15 5.83 us: extended(): lax.slice_in_dim(block, block.shape[dim] - width, None, axis=dim)]
  transfers between devices with their start and end apart: 26 -> 0, of which waited for: 11 -> 0; matrix products, arithmetic and copies ran while one was open for 36% -> 0% of each run, Pallas kernels for 0% -> 0%
where the time goes in v1:
time: 31.4 us; the launch traced here: 30.9 us
  Pallas kernels  23.2 us (74%)
  local copies, waits for them, and re-layouts  7.05 us (22%)
  between operations  0.68 us (2%)
    pallas_call x1, Pallas kernels, local(): pl.pallas_call(functools.partial(smooth_kernel, coarse.shape[1]), out_sha...  13.6 us
    pallas_call x1, Pallas kernels, local(): pl.pallas_call(functools.partial(exchange_kernel, groups, slabs), out_sha...  9.64 us
    unnamed x22, local copies, waits for them, and re-layouts  7.05 us

profile of v1, /device:TPU:13, one launch (start us, length us, event | category | flops | bytes accessed | tf_op | source)
XLA Modules:
  0.0 30.9 jit_solution(13481766386484031636)
XLA Ops:
  0.6 0.0 copy-start
  0.6 1.0 %copy-done = f32[32,32,128]{2,1,0:T(8,128)S(1)} copy-done((f32[32,32,128]{2,1,0:T(8,128)S(1)}, f32[32,32,128]{2,1,0:T(8,128)}, u32[]{:S(2)}) %copy-start) | copy-done | bytes 524312
  1.7 0.0 copy-start.5
  1.7 0.8 %copy-done.5 = bf16[128,128]{1,0:T(8,128)(2,1)S(1)} copy-done((bf16[128,128]{1,0:T(8,128)(2,1)S(1)}, bf16[128,128]{1,0:T(8,128)(2,1)}, u32[]{:S(2)}) %copy-start.5) | copy-done | bytes 32792
  2.4 0.0 copy-start.6
  2.4 0.7 %copy-done.6 = s32[4,4,16]{2,1,0:T(4,128)S(1)} copy-done((s32[4,4,16]{2,1,0:T(4,128)S(1)}, s32[4,4,16]{2,1,0:T(4,128)}, u32[]{:S(2)}) %copy-start.6) | copy-done | bytes 1048
  3.1 0.0 copy-start.7
  3.1 0.7 %copy-done.7 = s32[4,4,16]{2,1,0:T(4,128)S(1)} copy-done((s32[4,4,16]{2,1,0:T(4,128)S(1)}, s32[4,4,16]{2,1,0:T(4,128)}, u32[]{:S(2)}) %copy-start.7) | copy-done | bytes 1048
  3.8 0.0 copy-start.8
  3.8 0.7 %copy-done.8 = f32[1,4,512]{2,1,0:T(4,128)S(1)} copy-done((f32[1,4,512]{2,1,0:T(4,128)S(1)}, f32[1,4,512]{2,1,0:T(4,128)}, u32[]{:S(2)}) %copy-start.8) | copy-done | bytes 8216
  4.5 0.0 copy-start.9
  4.5 0.7 %copy-done.9 = s32[2,2,8]{2,1,0:T(2,128)S(1)} copy-done((s32[2,2,8]{2,1,0:T(2,128)S(1)}, s32[2,2,8]{2,1,0:T(2,128)}, u32[]{:S(2)}) %copy-start.9) | copy-done | bytes 152
  5.2 0.0 copy-start.1
  5.2 0.0 copy-start.4
  5.2 9.6 %exchange.1 = (f32[80,128]{1,0:T(8,128)S(1)}, f32[16,16,128]{2,1,0:T(8,128)S(1)}, f32[2,80,128]{2,1,0:T(8,128)S(1)}, f32[2,3,32,128]{3,2,1,0:T(8,128)S(1)}, f32[...) custom-call(f32[32,32,128]{2,1,0:T(8,128)S(1)} %copy-done, ...), custom_call_target="tpu_custom_call" | custom-call | tf_op jit(solution)/shard_map/exchange/pallas_call | solution.py:431
  14.9 0.0 copy-start.10
  14.9 0.0 copy-done.1
  14.9 0.0 copy-done.4
  14.9 0.6 %copy-done.10 = f32[16]{0:T(128)S(1)} copy-done((f32[16]{0:T(128)S(1)}, f32[16]{0:T(128)}, u32[]{:S(2)}) %copy-start.10) | copy-done | bytes 88
  15.5 0.0 copy-start.2
  15.5 0.9 %copy-done.2 = bf16[768,128]{1,0:T(8,128)(2,1)S(1)} copy-done((bf16[768,128]{1,0:T(8,128)(2,1)S(1)}, bf16[768,128]{1,0:T(8,128)(2,1)}, u32[]{:S(2)}) %copy-start.2) | copy-done | bytes 196632
  16.4 0.0 copy-start.3
  16.4 0.9 %copy-done.3 = bf16[128,768]{1,0:T(8,128)(2,1)S(1)} copy-done((bf16[128,768]{1,0:T(8,128)(2,1)S(1)}, bf16[128,768]{1,0:T(8,128)(2,1)}, u32[]{:S(2)}) %copy-start.3) | copy-done | bytes 196632
  17.4 13.6 %smooth.1 = (f32[16,16,64]{2,1,0:T(8,128)}, f32[32,32,128]{2,1,0:T(8,128)}) custom-call(f32[16]{0:T(128)S(1)} %copy-done.10, f32[32,32,128]{2,1,0:T(8,128)S(1)} %copy-done.1, f32[80,128]{1,0:T(8,128)S(1)} %get-tuple-element.10.msgz, f32[16,16,128]{2,1,0:T(8,128)S(1)} %get-tuple-element.11.s13, f32[2,80,128]{2,1,0:T(8,128)S(1)} %get-tuple-element.12.rz, ...), custom_call_target="tpu_custom_call" | custom-call | tf_op jit(solution)/shard_map/smooth/pallas_call | solution.py:450
Async XLA Ops:
  0.6 1.0 %copy-start = (f32[32,32,128]{2,1,0:T(8,128)S(1)}, f32[32,32,128]{2,1,0:T(8,128)}, u32[]{:S(2)}) copy-start(f32[32,32,128]{2,1,0:T(8,128)} %source.3) | copy-start | bytes 1572868
  1.7 0.8 %copy-start.5 = (bf16[128,128]{1,0:T(8,128)(2,1)S(1)}, bf16[128,128]{1,0:T(8,128)(2,1)}, u32[]{:S(2)}) copy-start(bf16[128,128]{1,0:T(8,128)(2,1)} %constant.8.clone.fold) | copy-start | bytes 98308
  2.4 0.7 %copy-start.6 = (s32[4,4,16]{2,1,0:T(4,128)S(1)}, s32[4,4,16]{2,1,0:T(4,128)}, u32[]{:S(2)}) copy-start(s32[4,4,16]{2,1,0:T(4,128)} %occ.1) | copy-start | bytes 3076
  3.1 0.7 %copy-start.7 = (s32[4,4,16]{2,1,0:T(4,128)S(1)}, s32[4,4,16]{2,1,0:T(4,128)}, u32[]{:S(2)}) copy-start(s32[4,4,16]{2,1,0:T(4,128)} %cls.1) | copy-start | bytes 3076
  3.8 0.7 %copy-start.8 = (f32[1,4,512]{2,1,0:T(4,128)S(1)}, f32[1,4,512]{2,1,0:T(4,128)}, u32[]{:S(2)}) copy-start(f32[1,4,512]{2,1,0:T(4,128)} %coarse.1) | copy-start | bytes 24580
  4.5 0.7 %copy-start.9 = (s32[2,2,8]{2,1,0:T(2,128)S(1)}, s32[2,2,8]{2,1,0:T(2,128)}, u32[]{:S(2)}) copy-start(s32[2,2,8]{2,1,0:T(2,128)} %par.1) | copy-start | bytes 388
  5.2 9.7 %copy-start.1 = (f32[32,32,128]{2,1,0:T(8,128)S(1)}, f32[32,32,128]{2,1,0:T(8,128)}, u32[]{:S(2)}) copy-start(f32[32,32,128]{2,1,0:T(8,128)} %source.3) | copy-start | bytes 1572868
  5.2 9.7 %copy-start.4 = (bf16[128,256]{1,0:T(8,128)(2,1)S(1)}, bf16[128,256]{1,0:T(8,128)(2,1)}, u32[]{:S(2)}) copy-start(bf16[128,256]{1,0:T(8,128)(2,1)} %constant.11.clone.fe) | copy-start | bytes 196612
  14.9 0.7 %copy-start.10 = (f32[16]{0:T(128)S(1)}, f32[16]{0:T(128)}, u32[]{:S(2)}) copy-start(f32[16]{0:T(128)} %table.1) | copy-start | bytes 196
  15.5 0.9 %copy-start.2 = (bf16[768,128]{1,0:T(8,128)(2,1)S(1)}, bf16[768,128]{1,0:T(8,128)(2,1)}, u32[]{:S(2)}) copy-start(bf16[768,128]{1,0:T(8,128)(2,1)} %constant.10.clone.fd) | copy-start | bytes 589828
  16.4 0.9 %copy-start.3 = (bf16[128,768]{1,0:T(8,128)(2,1)S(1)}, bf16[128,768]{1,0:T(8,128)(2,1)}, u32[]{:S(2)}) copy-start(bf16[128,768]{1,0:T(8,128)(2,1)} %constant.9.clone.fc) | copy-start | bytes 589828

commit v2 on v1

--- a/solution.py
+++ b/solution.py
@@ -12,7 +12,7 @@
 BF16 = jnp.bfloat16
 MESH = pl.DeviceIdType.MESH
 VM = pl.BlockSpec(memory_space=pltpu.VMEM)
-SM = pl.BlockSpec(memory_space=pltpu.SMEM)
+HB = pl.BlockSpec(memory_space=pltpu.HBM)
 
 NEAR = [(dx, dz) for dx in (-1, 0, 1) for dz in (-2, -1, 0, 1, 2) if (dx, dz) != (0, 0)]
 
@@ -35,9 +35,9 @@
 
 
 def exchange_kernel(
-    groups, slabs, source, occ, cls, par, coarse, fold,
-    msgz, s13, rz, rc, rf, rfx, rsrc, rs13,
-    msgx, xs13, send_sem, recv_sem,
+    groups, slabs, source_in, occ_in, cls_in, par_in, coarse_in, table_in, fold_in, fc_in, fd_in, fe_in,
+    source, tab, fc, fd, fe, msgz, s13, rz, rc, rf, rfx, rsrc, rs13,
+    occ, cls, par, coarse, table, fold, msgx, xs13, send_sem, recv_sem, load_sem,
 ):
     g = lax.axis_index("grp")
     s = lax.axis_index("slab")
@@ -47,6 +47,13 @@
     def exists(dx, dz):
         return (g + dx >= 0) & (g + dx < groups) & (s + dz >= 0) & (s + dz < slabs)
 
+    pairs = (
+        (source_in, source), (fold_in, fold), (coarse_in, coarse), (occ_in, occ), (cls_in, cls),
+        (par_in, par), (table_in, table), (fc_in, fc), (fd_in, fd), (fe_in, fe),
+    )
+    loads = [pltpu.make_async_copy(a, b, load_sem.at[i]) for i, (a, b) in enumerate(pairs)]
+    for load in loads:
+        load.start()
     for ref in (rz, rc, rf, rfx, rsrc, rs13):
         ref[...] = jnp.zeros(ref.shape, F32)
     barrier = pltpu.get_barrier_semaphore()
@@ -61,6 +68,10 @@
                 barrier, inc=1, device_id={"grp": g + dx, "slab": s + dz}, device_id_type=MESH
             )
 
+    for load in loads[:7]:
+        load.wait()
+    for i in range(table.shape[0]):
+        tab[i : i + 1, :] = jnp.full((1, 128), table[i], F32)
     lane = iota((8, 128), 1)
     for c in range(4):
         msgz[4 * c : 4 * c + 4, :] = coarse[0, :, 128 * c : 128 * c + 128]
@@ -138,6 +149,8 @@
         )
         made.append((copy, dx, dz))
         pl.when(exists(dx, dz))(copy.start)
+    for load in loads[7:]:
+        load.wait()
     for copy, dx, dz in made:
         pl.when(exists(-dx, -dz))(copy.wait_recv)
     for copy, dx, dz in made:
@@ -160,7 +173,7 @@
 
 
 def smooth_kernel(
-    slab_rows, table, source, msgz, s13, rz, rc, rf, rfx, rsrc, rs13, fc, fd, fe,
+    slab_rows, source, tab, fc, fd, fe, msgz, s13, rz, rc, rf, rfx, rsrc, rs13,
     middle, finest,
     pf, px, qx, pm, qm, occm, occf, v13, wr13, v14, wr14,
 ):
@@ -182,8 +195,9 @@
 
     def coefficients(occupied, label):
         weight = jnp.zeros_like(label)
-        for i in range(table.shape[0]):
-            weight = jnp.where(label == float(i), table[i], weight)
+        for i in range(tab.shape[0]):
+            value = jnp.concatenate([tab[i : i + 1, :]] * (label.shape[1] // 128), axis=1)
+            weight = jnp.where(label == float(i), jnp.broadcast_to(value, label.shape), weight)
         screen = 4.0 * weight
         inverse = occupied / (8.0 / 3.0 + screen * (8.0 / 27.0))
         p = inverse * (1.0 / 9.0)
@@ -431,26 +445,35 @@
     moved = pl.pallas_call(
         functools.partial(exchange_kernel, groups, slabs),
         out_shape=[
+            shape(nx, ny, nz), shape(screen_table.shape[0], 128),
+            *(jax.ShapeDtypeStruct(a.shape, BF16) for a in (fc, fd, fe)),
             shape(80, 128), shape(half, 16, 128), shape(2, 80, 128), shape(2, 3, 32, 128),
             shape(2, 16, 128), shape(2, 2, 8, 128), shape(2, 2, ny, nz), shape(2, 2, 16, 128),
         ],
-        in_specs=[VM] * 6,
-        out_specs=[VM] * 8,
+        in_specs=[HB] * 10,
+        out_specs=[VM] * 13,
         scratch_shapes=[
+            pltpu.VMEM(occupancy.shape, jnp.int32), pltpu.VMEM(classes.shape, jnp.int32),
+            pltpu.VMEM(parents.shape, jnp.int32), pltpu.VMEM(coarse.shape, F32),
+            pltpu.SMEM(screen_table.shape, F32), pltpu.VMEM(fold.shape, BF16),
             pltpu.VMEM((2, 32, 128), F32),
             pltpu.VMEM((2, 2, 16, 128), F32),
             pltpu.SemaphoreType.DMA((18,)),
             pltpu.SemaphoreType.DMA((18,)),
+            pltpu.SemaphoreType.DMA((10,)),
         ],
         compiler_params=pltpu.CompilerParams(
             collective_id=0, has_side_effects=True, vmem_limit_bytes=24 << 20
         ),
         name="exchange",
-    )(source, occupancy, classes, parents, coarse, fold)
+    )(*(
+        pltpu.with_memory_space_constraint(a, pltpu.HBM)
+        for a in (source, occupancy, classes, parents, coarse, screen_table, fold, fc, fd, fe)
+    ))
     return pl.pallas_call(
         functools.partial(smooth_kernel, coarse.shape[1]),
         out_shape=[shape(half, ny // 2, nz // 2), shape(nx, ny, nz)],
-        in_specs=[SM] + [VM] * 12,
+        in_specs=[VM] * 13,
         out_specs=[VM] * 2,
         scratch_shapes=[
             pltpu.VMEM((32, 256), F32),
@@ -464,7 +487,7 @@
         ],
         compiler_params=pltpu.CompilerParams(vmem_limit_bytes=32 << 20),
         name="smooth",
-    )(screen_table, source, *moved, fc, fd, fe)
+    )(*moved)
 
 
 def solution(mesh):

time: 31.4 us -> 23.6 us (0.75)
  local copies, waits for them, and re-layouts: 7.05 us -> 0 us
  Pallas kernels: 23.2 us -> 22.8 us
    unnamed x22 -> x0, local copies, waits for them, and re-layouts: 7.05 us -> none
    pallas_call x1, Pallas kernels: 13.6 us -> 13 us  [local(): pl.pallas_call(functools.partial(smooth_kernel, coarse.shape[1]), out_sha...]
where the time goes in v2:
time: 23.6 us; the launch traced here: 23.4 us
  Pallas kernels  22.8 us (97%)
  between operations  0.64 us (3%)
    pallas_call x1, Pallas kernels, local(): pl.pallas_call(functools.partial(smooth_kernel, coarse.shape[1]), out_sha...  13 us
    pallas_call x1, Pallas kernels, local(): pl.pallas_call(functools.partial(exchange_kernel, groups, slabs), out_sha...  9.75 us

profile of v2, /device:TPU:13, one launch (start us, length us, event | category | flops | bytes accessed | tf_op | source)
XLA Modules:
  0.0 23.4 jit_solution(12951566767744636733)
XLA Ops:
  0.6 9.7 %exchange.1 = (f32[32,32,128]{2,1,0:T(8,128)S(1)}, f32[16,128]{1,0:T(8,128)S(1)}, bf16[128,768]{1,0:T(8,128)(2,1)S(1)}, bf16[768,128]{1,0:T(8,128)(2,1)S(1)}, bf...) custom-call(f32[32,32,128]{2,1,0:T(8,128)} %source_in.1, ...), custom_call_target="tpu_custom_call" | custom-call | tf_op jit(solution)/shard_map/exchange/pallas_call | solution.py:445
  10.4 13.0 %smooth.1 = (f32[16,16,64]{2,1,0:T(8,128)}, f32[32,32,128]{2,1,0:T(8,128)}) custom-call(f32[32,32,128]{2,1,0:T(8,128)S(1)} %get-tuple-element.15.source, f32[16,128]{1,0:T(8,128)S(1)} %get-tuple-element.16.tab, bf16[128,768]{1,0:T(8,128)(2,1)S(1)} %get-tuple-element.17.fc, bf16[768,128]{1,0:T(8,128)(2,1)S(1)} %get-tuple-element.18.fd, ...), custom_call_target="tpu_custom_call" | custom-call | tf_op jit(solution)/shard_map/smooth/pallas_call | solution.py:473

commit v3 on v2

--- a/solution.py
+++ b/solution.py
@@ -390,7 +390,7 @@
                         v14[new, i, t, r] = out
             return now, after
 
-        lax.fori_loop(first + 4, last + 5, step, (pieces(first + 3), pieces(first + 4)))
+        lax.fori_loop(first + 4, last + 5, step, (pieces(first + 3), pieces(first + 4)), unroll=True)
 
 
 def constants():

time: 23.6 us -> 16.2 us (0.69)
  Pallas kernels: 22.8 us -> 15.4 us
    pallas_call x1, Pallas kernels: 13 us -> 5.69 us  [local(): pl.pallas_call(functools.partial(smooth_kernel, coarse.shape[1]), out_sha...]
where the time goes in v3:
time: 16.2 us; the launch traced here: 16.1 us
  Pallas kernels  15.4 us (95%)
  between operations  0.64 us (4%)
    pallas_call x1, Pallas kernels, local(): pl.pallas_call(functools.partial(exchange_kernel, groups, slabs), out_sha...  9.75 us
    pallas_call x1, Pallas kernels, local(): pl.pallas_call(functools.partial(smooth_kernel, coarse.shape[1]), out_sha...  5.69 us

profile of v3, /device:TPU:13, one launch (start us, length us, event | category | flops | bytes accessed | tf_op | source)
XLA Modules:
  0.0 16.1 jit_solution(11436983511367454375)
XLA Ops:
  0.6 9.7 %exchange.1 = (f32[32,32,128]{2,1,0:T(8,128)S(1)}, f32[16,128]{1,0:T(8,128)S(1)}, bf16[128,768]{1,0:T(8,128)(2,1)S(1)}, bf16[768,128]{1,0:T(8,128)(2,1)S(1)}, bf...) custom-call(f32[32,32,128]{2,1,0:T(8,128)} %source_in.1, ...), custom_call_target="tpu_custom_call" | custom-call | tf_op jit(solution)/shard_map/exchange/pallas_call | solution.py:445
  10.4 5.7 %smooth.1 = (f32[16,16,64]{2,1,0:T(8,128)}, f32[32,32,128]{2,1,0:T(8,128)}) custom-call(f32[32,32,128]{2,1,0:T(8,128)S(1)} %get-tuple-element.15.source, f32[16,128]{1,0:T(8,128)S(1)} %get-tuple-element.16.tab, bf16[128,768]{1,0:T(8,128)(2,1)S(1)} %get-tuple-element.17.fc, bf16[768,128]{1,0:T(8,128)(2,1)S(1)} %get-tuple-element.18.fd, ...), custom_call_target="tpu_custom_call" | custom-call | tf_op jit(solution)/shard_map/smooth/pallas_call | solution.py:473
